TPU v7x, 512 devices: a whole 4x4x16 slice. The times are simulated.
512 devices in a mesh: pair: 64 (over z, y), band: 8 (over x, core).
Axes of the slice: x: 4, y: 4, z: 16, core: 2. Of those that a mesh axis runs over, the one named last changes fastest.
Arguments:
- spectrum: bfloat16 [4096, 98304], P('band', 'pair'), may hold values from -6 to 6
- bessel_table: bfloat16 [4096, 512], P('band'), may hold values from -0.125 to 0.125
- interp_weights: bfloat16 [256, 8, 256, 512], P('pair', None, None, 'band'), may hold values from -0.09375 to 0.09375
- need_owner: int32 [256, 8], P('pair'), may hold values from 0 to 63, all different within a row; in each aligned block of 4 rows (0 to 3, 4 to 7, ...) at most 2 rows name the same one
- need_block: int32 [256, 8], P('pair'), may hold values from 0 to 11
Outputs:
- stress: float32 [256, 256, 128], P('pair', 'band')
Inputs may be any that keep to these rules, and one draw needn't show every extreme that they name: `need_owner`: each row names 8 different owners; among the 4 rows of one index of pair no owner is named by more than 2 rows, a bound that some block reaches.
All inputs are finite; a program needn't handle non-finite values.
Results may differ from a plain program's by a relative error of at most 0.0003.
Values sent between devices are 32-bit elements; how exact they have to be, the bound alone decides.
A program may use at most 64 MiB of HBM per device.

v0:
```python
import jax
import jax.numpy as jnp
from jax import lax
from jax.sharding import PartitionSpec as P

PB = 128
NB = 8


def shards(spectrum, bessel_table, interp_weights, need_owner, need_block):
    owners = lax.axis_size("pair")
    bands = lax.axis_size("band")
    radial = bessel_table.shape[1]
    radial_local = radial // bands
    pair_count = spectrum.shape[1]
    block_count = pair_count // PB
    tile_count = need_owner.shape[0]
    entries = tile_count * NB
    capacity = max(2, (2 * entries + owners - 1) // owners)
    kernel = lax.psum_scatter(
        lax.dot_general(
            bessel_table, spectrum, (((0,), (0,)), ((), ())), preferred_element_type=jnp.float32
        ),
        "band",
        scatter_dimension=0,
        tiled=True,
    )
    owner_flat = need_owner.reshape(entries)
    block_flat = need_block.reshape(entries)
    owner_iota = lax.broadcasted_iota(jnp.int32, (entries, owners), 1)
    named = (owner_flat[:, None] == owner_iota).astype(jnp.int32)
    slot_rank = jnp.sum((jnp.cumsum(named, axis=0) - named) * named, axis=1)
    slot_iota = lax.broadcasted_iota(jnp.int32, (entries, capacity), 1)
    slot_hot = (slot_rank[:, None] == slot_iota).astype(jnp.int32)
    wanted = jnp.sum(named[:, :, None] * slot_hot[:, None, :] * block_flat[:, None, None], axis=0)
    asked = lax.all_to_all(wanted, "pair", split_axis=0, concat_axis=0, tiled=True)
    kernel_view = kernel.reshape(radial_local, block_count, PB)
    outgoing = jnp.take(kernel_view, asked.reshape(owners * capacity), axis=1)
    outgoing = outgoing.reshape(radial_local, owners, capacity, PB)
    arrived = lax.all_to_all(outgoing, "pair", split_axis=1, concat_axis=1, tiled=True)
    arrived = arrived.reshape(radial_local, owners * capacity, PB)
    picked = jnp.take(arrived, owner_flat * capacity + slot_rank, axis=1)
    picked = picked.reshape(radial_local, tile_count, NB, PB)
    partial_value = jnp.einsum(
        "ijtr,rijp->itp",
        interp_weights.astype(jnp.float32),
        picked,
        precision=lax.Precision.HIGHEST,
    )
    return lax.psum_scatter(partial_value, "band", scatter_dimension=1, tiled=True)


def solution(mesh):
    return jax.shard_map(
        shards,
        mesh=mesh,
        in_specs=(
            P("band", "pair"),
            P("band", None),
            P("pair", None, None, "band"),
            P("pair", None),
            P("pair", None),
        ),
        out_specs=P("pair", "band", None),
        check_vma=False,
    )
```

profile of v0, /device:TPU:1, one launch (start us, length us, event | category | flops | bytes accessed | tf_op | source)
XLA Modules:
  0.0 353.6 jit_solution(2260693837872674361)
XLA Ops:
  6.5 1.4 copy-done
  7.9 3.7 %fusion.7 = f32[512,1536]{1,0:T(8,128)} fusion(bf16[512,512]{1,0:T(8,128)(2,1)} %param.6, bf16[512,1536]{1,0:T(8,128)(2,1)S(1)} %copy-done), kind=kOutput, calls=%fused_computation.27 | convolution fusion | flops 805306368 | bytes 5242880 | tf_op jit(solution)/shard_map/dot_general | solution.py:21
  11.7 0.0 reduce-scatter.2.cloned.1.call-update
  11.7 0.1 reshape.135
  11.8 0.1 mul.51
  11.9 0.1 fusion.3
  11.9 0.1 reduce_window_sum.11
  12.0 0.2 select_reduce_fusion
  12.2 0.1 multiply_reduce_fusion
  12.3 0.1 copy.19
  12.4 32.5 %all_to_all.14 = s32[64,1,2]{2,1,0:T(1,128)S(1)} all-to-all(s32[64,1,2]{2,1,0:T(1,128)S(1)} %copy.19), channel_id=1, replica_groups=mesh['pair'=64,'band'=8] {'pair'}, dimensions={0} | all-to-all | bytes 1024 | tf_op jit(solution)/shard_map/all_to_all | solution.py:36
  44.9 0.5 broadcast.106
  45.4 0.7 reduce.3
  46.2 0.1 reshape.138
  46.3 0.1 copy.20
  46.4 0.1 copy.21
  46.5 12.4 %reduce-scatter.2.cloned.1.call-done = f32[64,1536]{1,0:T(8,128)} async-done(((f32[512,1536]{1,0:T(8,128)}), f32[64,1536]{1,0:T(8,128)}) %reduce-scatter.2.cloned.1.call-update) | async-done | bytes 393232 | tf_op jit(solution)/shard_map/reduce_scatter | solution.py:20
  58.9 1.0 copy_bitcast_fusion
  60.0 2.8 gather_fusion
  62.7 4.5 %broadcast_select_fusion = f32[64,64,2,128]{3,0,2,1:T(8,128)} fusion(f32[64,64,2,128]{3,0,2,1:T(8,128)} %bitcast.32, pred[64,2]{1,0:T(8,128)(4,1)S(1)} %copy.21), kind=kLoop, calls=%fused_computation.2 | loop fusion | flops 1048576 | bytes 8388736 | tf_op jit(solution)/shard_map/jit(_take)/select_n | solution.py:38
  67.2 14.4 %all-to-all-start.1 = ((f32[64,64,2,128]{3,0,2,1:T(8,128)}), f32[64,64,2,128]{3,0,2,1:T(8,128)}, u32[]{:S(2)}, u32[]{:S(2)}) async-start(f32[64,64,2,128]{3,0,2,1:T(8,128)} %broadcast_select_fusion), calls=%async_computation.2 | async-start | bytes 8388608 | tf_op jit(solution)/shard_map/all_to_all | solution.py:40
  81.6 0.0 all-reduce.3.cloned.1.call-start
  81.6 0.1 reduce_sum.23
  81.7 0.1 mul.54
  81.8 182.8 %all-to-all-done.1 = f32[64,64,2,128]{3,0,2,1:T(8,128)} async-done(((f32[64,64,2,128]{3,0,2,1:T(8,128)}), f32[64,64,2,128]{3,0,2,1:T(8,128)}, u32[]{:S(2)}, u32[]{:S(2)}) %all-to-all-start.1) | async-done | bytes 4194336 | tf_op jit(solution)/shard_map/all_to_all | solution.py:40
  264.6 2.8 gather_fusion.1
  267.4 2.3 convolution_bitcast_fusion
  269.7 1.0 copy.23
  270.8 1.3 dynamic-slice
  272.7 72.5 %all-reduce.3.cloned.1.call-done = f32[4,256,128]{2,0,1:T(4,128)} async-done(((f32[4,256,128]{2,0,1:T(4,128)}), f32[4,256,128]{2,0,1:T(4,128)}) %all-reduce.3.cloned.1.call-update) | async-done | bytes 524304
  345.2 0.8 constant_dynamic-slice_fusion
  346.1 0.6 copy.24
  (15 shorter events, 0.1 us)
Async XLA Ops:
  6.5 1.4 copy-start
  6.5 5.1 %copy-start.1 = (s32[4,8]{1,0:T(4,128)S(1)}, s32[4,8]{1,0:T(4,128)}, u32[]{:S(2)}) copy-start(s32[4,8]{1,0:T(4,128)} %param.8) | copy-start | bytes 388
  6.5 5.2 %copy-start.2 = (s32[4,8]{1,0:T(4,128)S(1)}, s32[4,8]{1,0:T(4,128)}, u32[]{:S(2)}) copy-start(s32[4,8]{1,0:T(4,128)} %param.9) | copy-start | bytes 388
  6.5 52.4 %reduce-scatter.2.cloned.1.call-start = ((), (), s32[]{:S(2)}) async-start(), calls=%async_computation.3 | async-start | bytes 3538944 | tf_op jit(solution)/shard_map/reduce_scatter | solution.py:20
  67.2 197.4 %all-to-all-start.1 = ((f32[64,64,2,128]{3,0,2,1:T(8,128)}), f32[64,64,2,128]{3,0,2,1:T(8,128)}, u32[]{:S(2)}, u32[]{:S(2)}) async-start(f32[64,64,2,128]{3,0,2,1:T(8,128)} %broadcast_select_fusion), calls=%async_computation.2 | async-start | bytes 8388608 | tf_op jit(solution)/shard_map/all_to_all | solution.py:40
  81.6 263.7 %all-reduce.3.cloned.1.call-start = ((), (), s32[]{:S(2)}) async-start(), calls=%async_computation.4 | async-start | bytes 1048576
Sparse Core Ops, SparseCore 0:
  11.8 47.0 reduce-scatter.1
  270.9 74.2 all-reduce.2
where the time goes:
time: 355 us; the launch traced here: 354 us
  waiting for transfers between devices  268 us (75%)
  blocking collectives  32.5 us (9%)
  starting transfers between devices  14.4 us (4%)
  between operations  14.2 us (4%)
  local copies, waits for them, and re-layouts  13 us (4%)
  matrix products  6.05 us (2%)
  other arithmetic  5.65 us (2%)
    all_to_all x1, waiting for transfers between devices, shards(): lax.all_to_all(outgoing, 'pair', split_axis=1, concat_axis=1, tiled=True)  183 us
    unnamed x3, waiting for transfers between devices  72.6 us
    all_to_all x1, blocking collectives, shards(): lax.all_to_all(wanted, 'pair', split_axis=0, concat_axis=0, tiled=True)  32.5 us
    all_to_all x1, starting transfers between devices, shards(): lax.all_to_all(outgoing, 'pair', split_axis=1, concat_axis=1, tiled=True)  14.4 us
    reduce_scatter x1, waiting for transfers between devices, shards(): lax.psum_scatter(lax.dot_general(bessel_table, spectrum, (((0,), (0,)), (...  12.4 us
  transfers between devices with their start and end apart: 3, of which 3 were waited for; matrix products, arithmetic and copies ran while one was open for 1% of the time, Pallas kernels for 0%

commit v1 on v0

v1 whole, which is shorter than its diff:
```python
import functools

import jax
import jax.numpy as jnp
from jax import lax
from jax.experimental import pallas as pl
from jax.experimental.pallas import tpu as pltpu
from jax.sharding import PartitionSpec as P

PB = 128
NY = 4
CH = 16
MESH = pl.DeviceIdType.MESH
F32 = jnp.float32
BF16 = jnp.bfloat16


def kernel(
    sizes,
    table_in, spec_in, weights_in, owner_in, block_in,
    out,
    table, spec, weights, table_t, weights_t,
    part, core_in, band_in, ring, desk, picked, slots, blocks, share, share_in,
    wants, wants_s, place_s,
    load_sem, core_send, core_recv, x_send, x_recv, z_send, z_recv,
    want_send, want_recv, want_local, y_send, y_recv, f_send, f_recv,
):
    nx, nz, nq, nb, nt, nj, tri = sizes
    bands = 2 * nx
    half = nz // 2
    pair = lax.axis_index("pair")
    band = lax.axis_index("band")
    z, y = pair // NY, lax.rem(pair, NY)
    x, core = band // 2, lax.rem(band, 2)
    rows = tri // bands

    def x_peer(i):
        return (pair, lax.rem(x + i, nx) * 2 + core)

    def y_peer(i):
        return (z * NY + lax.rem(y + i, NY), band)

    def band_peer(i):
        return (pair, lax.rem(band + i, bands))

    sibling = (pair, x * 2 + 1 - core)
    up = (lax.rem(z + 1, nz) * NY + y, band)
    down = (lax.rem(z + nz - 1, nz) * NY + y, band)

    loads = [
        pltpu.make_async_copy(src, dst, load_sem.at[i])
        for i, (src, dst) in enumerate(((table_in, table), (spec_in, spec), (weights_in, weights)))
    ]
    for load in loads:
        load.start()

    barrier = pltpu.get_barrier_semaphore()
    partners = [band_peer(i) for i in range(1, bands)]
    partners += [y_peer(i) for i in range(1, NY)] + [up, down]
    for partner in partners:
        pl.semaphore_signal(barrier, inc=1, device_id=partner, device_id_type=MESH)

    loads[0].wait()
    turned = table[...].T
    for b in range(bands):
        for q in range(nq):
            at = b * nq * CH + q * CH
            table_t[q, b % 2, b // 2] = turned[at : at + CH]
    loads[1].wait()

    def hankel(q):
        left = table_t[q].reshape(bands * CH, table_t.shape[-1])
        product = jnp.dot(left, spec[...], preferred_element_type=F32)
        part[q] = product.reshape(2, nx, CH, nb * PB)

    def core_copy(q):
        return pltpu.make_async_remote_copy(
            part.at[q, 1 - core], core_in.at[q], core_send.at[q], core_recv.at[q],
            device_id=sibling, device_id_type=MESH,
        )

    def x_copy(q, i):
        return pltpu.make_async_remote_copy(
            part.at[q, core, lax.rem(x + i, nx)], band_in.at[q, nx - i],
            x_send.at[q, i], x_recv.at[q, nx - i],
            device_id=x_peer(i), device_id_type=MESH,
        )

    def across_cores(q):
        core_copy(q).wait_recv()
        part[q, core] = part[q, core] + core_in[q]
        for i in range(1, nx):
            x_copy(q, i).start()

    def own_rows(q):
        for i in range(1, nx):
            pltpu.make_async_copy(band_in.at[q, i], band_in.at[q, i], x_recv.at[q, i]).wait()
        total = part[q, core, x]
        for i in range(1, nx):
            total = total + band_in[q, i]
        for b in range(nb):
            ring[0, q, b] = total[:, b * PB : (b + 1) * PB]

    hankel(0)
    pl.semaphore_wait(barrier, len(partners))
    core_copy(0).start()

    lane = lax.broadcasted_iota(jnp.int32, (8, PB), 1)
    row = lax.broadcasted_iota(jnp.int32, (8, PB), 0)
    zero = jnp.zeros((8, PB), jnp.int32)

    def want_row(t, carry):
        first, second, count = carry
        for j in range(nj):
            hit = lane == owner_in[t, j]
            number = block_in[t, j]
            first = jnp.where(hit & (count == 0), number, first)
            second = jnp.where(hit & (count == 1), number, second)
            count = count + hit.astype(jnp.int32)
        return first, second, count

    first, second, _ = lax.fori_loop(0, nt, want_row, (zero, zero, zero))
    wants[0] = jnp.where(row == 0, first, jnp.where(row == 1, second, 0))

    def want_copy(i):
        return pltpu.make_async_remote_copy(
            wants.at[0], wants.at[NY - i], want_send.at[i], want_recv.at[NY - i],
            device_id=y_peer(i), device_id_type=MESH,
        )

    for i in range(1, NY):
        want_copy(i).start()

    for q in range(1, nq):
        hankel(q)
        core_copy(q).start()
        across_cores(q - 1)
    across_cores(nq - 1)

    def place_row(t, carry):
        for j in range(nj):
            who = owner_in[t, j]
            rank = jnp.int32(0)
            for u in range(nt - 1):
                for k in range(nj):
                    same = (owner_in[u, k] == who) & (u < t)
                    rank = rank + same.astype(jnp.int32)
            dz = lax.rem(z - who // NY + nz, nz)
            dy = lax.rem(lax.rem(who, NY) - y + NY, NY)
            spot = jnp.where(
                dz == 0, 0, jnp.where(dz == half, 1, jnp.where(dz < half, 2 * dz, 2 * (nz - dz) + 1))
            )
            place_s[t * nj + j] = (dy * nz + spot) * 2 + jnp.minimum(rank, 1)
        return carry

    lax.fori_loop(0, nt, place_row, 0)

    loads[2].wait()

    def turn(t, carry):
        weights_t[t] = weights[t].reshape(weights_t.shape[2], tri).T
        return carry

    lax.fori_loop(0, nt, turn, 0)

    for i in range(1, NY):
        pltpu.make_async_copy(wants.at[i], wants.at[i], want_recv.at[i]).wait()
    to_scalar = pltpu.make_async_copy(wants, wants_s, want_local)
    to_scalar.start()
    to_scalar.wait()

    def z_copy(way, d, q):
        here = d if way == 0 else lax.rem(nz - d, nz)
        there = d + 1 if way == 0 else nz - d - 1
        return pltpu.make_async_remote_copy(
            ring.at[here, q], ring.at[there, q], z_send.at[way], z_recv.at[way, d + 1, q],
            device_id=up if way == 0 else down, device_id_type=MESH,
        )

    def z_wait(way, d, q):
        here = d if way == 0 else nz - d
        pltpu.make_async_copy(ring.at[here, q], ring.at[here, q], z_recv.at[way, d, q]).wait()

    def y_copy(i, q, spot, count):
        at = pl.ds(spot * 2, count * 2)
        to = pl.ds((NY - i) * nz * 2 + spot * 2, count * 2)
        return pltpu.make_async_remote_copy(
            picked.at[q, i, at], slots.at[q, to], y_send, y_recv.at[q],
            device_id=y_peer(i), device_id_type=MESH,
        )

    def pick(q, spot, froms):
        for n, here in enumerate(froms):
            who = lax.rem(z - here + nz, nz) * NY + y
            desk[n] = ring[here, q]
            for i in range(NY):
                for s in range(2):
                    rows_of = desk[n, wants_s[i, s, who]]
                    if i == 0:
                        slots[q, (spot + n) * 2 + s] = rows_of
                    else:
                        picked[q, i, (spot + n) * 2 + s] = rows_of
        for i in range(1, NY):
            y_copy(i, q, spot, len(froms)).start()

    group = 2
    for g in range(nq // group):
        chunks = range(g * group, (g + 1) * group)
        for q in chunks:
            own_rows(q)
            z_copy(0, 0, q).start()
            z_copy(1, 0, q).start()
        for q in chunks:
            pick(q, 0, (0,))

        def step(d, carry):
            for q in chunks:
                for way in range(2):
                    z_wait(way, d, q)
                    z_copy(way, d, q).start()
            for q in chunks:
                pick(q, 2 * d, (d, nz - d))
            return carry

        lax.fori_loop(1, half - 1, step, 0)
        d = half - 1
        for q in chunks:
            for way in range(2):
                z_wait(way, d, q)
                if way == q % 2:
                    z_copy(way, d, q).start()
        for q in chunks:
            pick(q, 2 * d, (d, nz - d))
        for q in chunks:
            z_wait(q % 2, half, q)
            pick(q, 1, (half,))

    for q in range(nq):
        whole = slots.at[q, pl.ds(nz * 2, (NY - 1) * nz * 2)]
        pltpu.make_async_copy(whole, whole, y_recv.at[q]).wait()

    def tile(t, carry):
        for j in range(nj):
            place = place_s[t * nj + j]
            for q in range(nq):
                value = slots[q, place]
                high = value.astype(BF16)
                low = (value - high.astype(F32)).astype(BF16)
                at = (j * nq + q) * CH
                blocks[t, at : at + CH, :PB] = high
                blocks[t, at : at + CH, PB:] = low
        both = jnp.dot(weights_t[t], blocks[t], preferred_element_type=F32)
        total = both[:, :PB] + both[:, PB:]
        for b in range(bands):
            share[b, t] = total[b * rows : (b + 1) * rows]
        return carry

    lax.fori_loop(0, nt, tile, 0)

    def f_copy(i):
        return pltpu.make_async_remote_copy(
            share.at[lax.rem(band + i, bands)], share_in.at[bands - i], f_send.at[i], f_recv.at[bands - i],
            device_id=band_peer(i), device_id_type=MESH,
        )

    for i in range(1, bands):
        f_copy(i).start()
    total = share[band]
    for i in range(1, bands):
        pltpu.make_async_copy(share_in.at[i], share_in.at[i], f_recv.at[i]).wait()
        total = total + share_in[i]
    out[...] = total

    for q in range(nq):
        core_copy(q).wait_send()
        for i in range(1, nx):
            x_copy(q, i).wait_send()
    for i in range(1, NY):
        want_copy(i).wait_send()
    for i in range(1, bands):
        f_copy(i).wait_send()
    sent = (nz - 1) * nq // 2
    for way in range(2):
        for i in range(sent // nq):
            pltpu.make_async_copy(ring.at[i], ring.at[i], z_send.at[way]).wait()
        if sent % nq:
            some = ring.at[0, pl.ds(0, sent % nq)]
            pltpu.make_async_copy(some, some, z_send.at[way]).wait()
    whole = picked.at[:, pl.ds(1, NY - 1)]
    pltpu.make_async_copy(whole, whole, y_send).wait()


def shards(spectrum, bessel_table, interp_weights, need_owner, need_block):
    bands = lax.axis_size("band")
    nz = lax.axis_size("pair") // NY
    nx = bands // 2
    depth, radial = bessel_table.shape
    nb = spectrum.shape[1] // PB
    nt, nj, tri, local = interp_weights.shape
    nq = local // CH
    sizes = (nx, nz, nq, nb, nt, nj, tri)
    weights = jnp.swapaxes(interp_weights, 2, 3)
    dma = pltpu.SemaphoreType.DMA
    return pl.pallas_call(
        functools.partial(kernel, sizes),
        out_shape=jax.ShapeDtypeStruct((nt, tri // bands, PB), F32),
        in_specs=[pl.BlockSpec(memory_space=pl.ANY)] * 3
        + [pl.BlockSpec(memory_space=pltpu.SMEM)] * 2,
        out_specs=pl.BlockSpec(memory_space=pltpu.VMEM),
        scratch_shapes=[
            pltpu.VMEM((depth, radial), BF16),
            pltpu.VMEM(spectrum.shape, BF16),
            pltpu.VMEM(weights.shape, BF16),
            pltpu.VMEM((nq, 2, nx, CH, depth), BF16),
            pltpu.VMEM((nt, tri, nj * local), BF16),
            pltpu.VMEM((nq, 2, nx, CH, nb * PB), F32),
            pltpu.VMEM((nq, nx, CH, nb * PB), F32),
            pltpu.VMEM((nq, nx, CH, nb * PB), F32),
            pltpu.VMEM((nz, nq, nb, CH, PB), F32),
            pltpu.VMEM((2, nb, CH, PB), F32),
            pltpu.VMEM((nq, NY, nz * 2, CH, PB), F32),
            pltpu.VMEM((nq, NY * nz * 2, CH, PB), F32),
            pltpu.VMEM((nt, nj * local, 2 * PB), BF16),
            pltpu.VMEM((bands, nt, tri // bands, PB), F32),
            pltpu.VMEM((bands, nt, tri // bands, PB), F32),
            pltpu.VMEM((NY, 8, PB), jnp.int32),
            pltpu.SMEM((NY, 8, PB), jnp.int32),
            pltpu.SMEM((nt * nj,), jnp.int32),
            dma((3,)),
            dma((nq,)),
            dma((nq,)),
            dma((nq, nx)),
            dma((nq, nx)),
            dma((2,)),
            dma((2, nz // 2 + 1, nq)),
            dma((NY,)),
            dma((NY,)),
            dma,
            dma,
            dma((nq,)),
            dma((bands,)),
            dma((bands,)),
        ],
        compiler_params=pltpu.CompilerParams(
            collective_id=0, has_side_effects=True, vmem_limit_bytes=56 * 1024 * 1024
        ),
        cost_estimate=pl.CostEstimate(flops=1 << 30, bytes_accessed=4 << 20, transcendentals=0),
    )(bessel_table, spectrum, weights, need_owner, need_block)


def solution(mesh):
    return jax.shard_map(
        shards,
        mesh=mesh,
        in_specs=(
            P("band", "pair"),
            P("band", None),
            P("pair", None, None, "band"),
            P("pair", None),
            P("pair", None),
        ),
        out_specs=P("pair", "band", None),
        check_vma=False,
    )
```

time: 355 us -> 116 us (0.33)
  waiting for transfers between devices: 268 us -> 0 us
  Pallas kernels: 0 us -> 114 us
  blocking collectives: 32.5 us -> 0 us
  starting transfers between devices: 14.4 us -> 0 us
  between operations: 14.2 us -> 0.01 us
  local copies, waits for them, and re-layouts: 13 us -> 1.47 us
  matrix products: 6.05 us -> 0 us
  other arithmetic: 5.65 us -> 0 us
    all_to_all x1 -> x0, waiting for transfers between devices: 183 us -> none  [shards(): lax.all_to_all(outgoing, 'pair', split_axis=1, concat_axis=1, tiled=True)]
    pallas_call x0 -> x1, Pallas kernels: none -> 114 us  [shards(): pl.pallas_call(functools.partial(kernel, sizes), out_shape=jax.ShapeDtype...]
    unnamed x3 -> x0, waiting for transfers between devices: 72.6 us -> none
    all_to_all x1 -> x0, blocking collectives: 32.5 us -> none  [shards(): lax.all_to_all(wanted, 'pair', split_axis=0, concat_axis=0, tiled=True)]
    all_to_all x1 -> x0, starting transfers between devices: 14.4 us -> none  [shards(): lax.all_to_all(outgoing, 'pair', split_axis=1, concat_axis=1, tiled=True)]
    reduce_scatter x1 -> x0, waiting for transfers between devices: 12.4 us -> none  [shards(): lax.psum_scatter(lax.dot_general(bessel_table, spectrum, (((0,), (0,)), (...]
    dot_general x2 -> x0, matrix products: 6.05 us -> none  [the longest x1 3.71 us: shards(): lax.dot_general(bessel_table, spectrum, (((0,), (0,)), ((), ())), preferr...]
    gather x2 -> x0, local copies, waits for them, and re-layouts: 5.59 us -> none  [the longest x1 2.8 us: shards(): picked = jnp.take(arrived, owner_flat * capacity + slot_rank, axis=1)]
  transfers between devices with their start and end apart: 3 -> 0, of which waited for: 3 -> 0; matrix products, arithmetic and copies ran while one was open for 1% -> 0% of each run, Pallas kernels for 0% -> 0%
where the time goes in v1:
time: 116 us
  Pallas kernels  114 us (98%)
  local copies, waits for them, and re-layouts  1.47 us (1%)
    pallas_call x1, Pallas kernels, shards(): pl.pallas_call(functools.partial(kernel, sizes), out_shape=jax.ShapeDtype...  114 us

profile of v1, /device:TPU:1, one launch (start us, length us, event | category | flops | bytes accessed | tf_op | source)
XLA Modules:
  0.0 115.7 jit_solution(8460808834425544916)
XLA Ops:
  0.0 114.2 %shard_map.55 = f32[4,32,128]{2,1,0:T(8,128)} custom-call(bf16[512,512]{1,0:T(8,128)(2,1)} %table_in.1, bf16[512,1536]{1,0:T(8,128)(2,1)} %spec_in.1, bf16[4,8,64,256]{3,2,1,0:T(8,128)(2,1)} %bitcast.1, s32[4,8]{1,0:T(4,128)} %owner_in.1, s32[4,8]{1,0:T(4,128)} %block_in.1), custom_call_target="tpu_custom_call" | custom-call | flops 1073741824 | bytes 4194304 | tf_op jit(solution)/shard_map/pallas_call | solution.py:304
  114.3 1.5 %copy.7 = f32[4,32,128]{2,1,0:T(8,128)} copy(f32[4,32,128]{2,1,0:T(8,128)} %shard_map.55) | data formatting | bytes 131072

commit v2 on v0

v2 whole, which is shorter than its diff:
```python
import functools

import jax
import jax.numpy as jnp
from jax import lax
from jax.experimental import pallas as pl
from jax.experimental.pallas import tpu as pltpu
from jax.sharding import PartitionSpec as P

PB = 128
NY = 4
CH = 8
UNIT = 16
GROUP = 4
LAG = 3
PACE = 2
MESH = pl.DeviceIdType.MESH
F32 = jnp.float32
BF16 = jnp.bfloat16


def z_order(nz, nq):
    half = nz // 2
    ready = [{(0, c): PACE * c for c in range(nq)} for _ in range(2)]
    ends = [{}, {}]
    order, time = [], 0
    while any(ready) or any(ends):
        slot = []
        for way in range(2):
            now = [k for k, at in ready[way].items() if at <= time]
            if now:
                d, c = min(now, key=lambda k: (k[1] // GROUP, k[0], k[1]))
                del ready[way][d, c]
                slot.append(("send", way, d, c))
                goes_on = d + 1 < half - 1 or (d + 1 == half - 1 and c % 2 == way)
                (ready if goes_on else ends)[way][d + 1, c] = time + LAG
            for d, c in sorted(k for k, at in ends[way].items() if at <= time):
                del ends[way][d, c]
                slot.append(("end", way, d, c))
        order.append(slot)
        time += 1
    return order


def kernel(
    sizes,
    table_in, spec_in, weights_in, owner_in, block_in,
    out,
    table, spec, weights, table_t, weights_t,
    part, core_in, band_in, ring, desk, picked, slots_0, slots_1, blocks, early,
    share, share_core, share_x,
    wants, wants_s, place_s,
    load_sem, core_send, core_recv, x_send, x_recv, z_send, z_recv,
    want_send, want_recv, want_local, y_send, y_recv,
    fc_send, fc_recv, fx_send, fx_recv,
):
    nx, nz, nq, nb, nt, nj, tri = sizes
    bands = 2 * nx
    units = nq * CH // UNIT
    per_unit = UNIT // CH
    groups = nq // GROUP
    slots = (slots_0, slots_1)
    pair = lax.axis_index("pair")
    band = lax.axis_index("band")
    z, y = pair // NY, lax.rem(pair, NY)
    x, core = band // 2, lax.rem(band, 2)
    rows = tri // bands

    def x_peer(i):
        return (pair, lax.rem(x + i, nx) * 2 + core)

    def y_peer(i):
        return (z * NY + lax.rem(y + i, NY), band)

    sibling = (pair, x * 2 + 1 - core)
    up = (lax.rem(z + 1, nz) * NY + y, band)
    down = (lax.rem(z + nz - 1, nz) * NY + y, band)

    barrier = pltpu.get_barrier_semaphore()
    partners = [x_peer(i) for i in range(1, nx)] + [y_peer(i) for i in range(1, NY)] + [up, down, sibling]
    for partner in partners:
        pl.semaphore_signal(barrier, inc=1, device_id=partner, device_id_type=MESH)

    loads = [
        pltpu.make_async_copy(src, dst, load_sem.at[i])
        for i, (src, dst) in enumerate(((table_in, table), (spec_in, spec), (weights_in, weights)))
    ]
    for load in loads:
        load.start()

    lane = lax.broadcasted_iota(jnp.int32, (8, PB), 1)
    row = lax.broadcasted_iota(jnp.int32, (8, PB), 0)
    zero = jnp.zeros((8, PB), jnp.int32)

    def want_row(t, carry):
        first, second, count = carry
        for j in range(nj):
            hit = lane == owner_in[t, j]
            number = block_in[t, j]
            first = jnp.where(hit & (count == 0), number, first)
            second = jnp.where(hit & (count == 1), number, second)
            count = count + hit.astype(jnp.int32)
        return first, second, count

    first, second, _ = lax.fori_loop(0, nt, want_row, (zero, zero, zero))
    wants[0] = jnp.where(row == 0, first, jnp.where(row == 1, second, 0))

    loads[0].wait()
    turned = table[...].T
    for b in range(bands):
        for u in range(units):
            at = (b * units + u) * UNIT
            table_t[u, b % 2, b // 2] = turned[at : at + UNIT]
    loads[1].wait()

    def hankel(u):
        left = table_t[u].reshape(bands * UNIT, table_t.shape[-1])
        product = jnp.dot(left, spec[...], preferred_element_type=F32)
        part[u] = product.reshape(2, nx, UNIT, nb * PB)

    def core_copy(u):
        return pltpu.make_async_remote_copy(
            part.at[u, 1 - core], core_in.at[u], core_send.at[u], core_recv.at[u],
            device_id=sibling, device_id_type=MESH,
        )

    def x_copy(c, i):
        some = pl.ds(c % per_unit * CH, CH)
        return pltpu.make_async_remote_copy(
            part.at[c // per_unit, core, lax.rem(x + i, nx), some], band_in.at[c, nx - i],
            x_send.at[c, i], x_recv.at[c, nx - i],
            device_id=x_peer(i), device_id_type=MESH,
        )

    def across_cores(u):
        core_copy(u).wait_recv()
        part[u, core] = part[u, core] + core_in[u]
        for c in range(u * per_unit, (u + 1) * per_unit):
            for i in range(1, nx):
                x_copy(c, i).start()

    def own_rows(c):
        for i in range(1, nx):
            pltpu.make_async_copy(band_in.at[c, i], band_in.at[c, i], x_recv.at[c, i]).wait()
        at = c % per_unit * CH
        total = part[c // per_unit, core, x, at : at + CH]
        for i in range(1, nx):
            total = total + band_in[c, i]
        for b in range(nb):
            ring[0, c, b] = total[:, b * PB : (b + 1) * PB]

    def want_copy(i):
        return pltpu.make_async_remote_copy(
            wants.at[0], wants.at[NY - i], want_send.at[i], want_recv.at[NY - i],
            device_id=y_peer(i), device_id_type=MESH,
        )

    hankel(0)
    pl.semaphore_wait(barrier, len(partners))
    core_copy(0).start()
    for i in range(1, NY):
        want_copy(i).start()
    for u in range(1, units):
        hankel(u)
        core_copy(u).start()
        across_cores(u - 1)
    across_cores(units - 1)

    to_scalar = pltpu.make_async_copy(wants, wants_s, want_local)
    for i in range(1, NY):
        pltpu.make_async_copy(wants.at[i], wants.at[i], want_recv.at[i]).wait()
    to_scalar.start()

    def place_row(t, carry):
        for j in range(nj):
            who = owner_in[t, j]
            rank = jnp.int32(0)
            for u in range(nt - 1):
                for k in range(nj):
                    same = (owner_in[u, k] == who) & (u < t)
                    rank = rank + same.astype(jnp.int32)
            dz = lax.rem(z - who // NY + nz, nz)
            dy = lax.rem(lax.rem(who, NY) - y + NY, NY)
            place_s[t * nj + j] = (dy * nz + dz) * 2 + jnp.minimum(rank, 1)
        return carry

    def turn(t, carry):
        for g in range(groups):
            at = g * GROUP * CH
            some = weights[t, :, at : at + GROUP * CH, :]
            weights_t[g, t] = some.reshape(nj * GROUP * CH, tri).T
        return carry

    def z_copy(way, d, c):
        here = d if way == 0 else (nz - d) % nz
        there = d + 1 if way == 0 else nz - d - 1
        return pltpu.make_async_remote_copy(
            ring.at[here, c], ring.at[there, c], z_send.at[way], z_recv.at[way, d + 1, c],
            device_id=up if way == 0 else down, device_id_type=MESH,
        )

    def z_wait(way, d, c):
        here = d if way == 0 else nz - d
        pltpu.make_async_copy(ring.at[here, c], ring.at[here, c], z_recv.at[way, d, c]).wait()

    def y_copy(i, g, here):
        return pltpu.make_async_remote_copy(
            picked.at[g, i, pl.ds(here * 2, 2)], slots[g].at[pl.ds(((NY - i) * nz + here) * 2, 2)],
            y_send, y_recv.at[g],
            device_id=y_peer(i), device_id_type=MESH,
        )

    done = {}

    def pick(here, c):
        g = c // GROUP
        at = c % GROUP * CH
        n = len(done) % 2
        done[here, c] = True
        desk[n] = ring[here, c]
        who = lax.rem(z + nz - here, nz) * NY + y
        for i in range(NY):
            for s in range(2):
                rows_of = desk[n, wants_s[i, s, who]]
                if i == 0:
                    slots[g][here * 2 + s, at : at + CH] = rows_of
                else:
                    picked[g, i, here * 2 + s, at : at + CH] = rows_of
        if all((here, k) in done for k in range(g * GROUP, (g + 1) * GROUP)):
            for i in range(1, NY):
                y_copy(i, g, here).start()

    def product(g, t):
        for j in range(nj):
            value = slots[g][place_s[t * nj + j]]
            high = value.astype(BF16)
            low = (value - high.astype(F32)).astype(BF16)
            at = j * GROUP * CH
            blocks[g, t, at : at + GROUP * CH, :PB] = high
            blocks[g, t, at : at + GROUP * CH, PB:] = low
        both = jnp.dot(weights_t[g, t], blocks[g, t], preferred_element_type=F32)
        return both[:, :PB] + both[:, PB:]

    def y_wait(g):
        whole = slots[g].at[pl.ds(nz * 2, (NY - 1) * nz * 2)]
        pltpu.make_async_copy(whole, whole, y_recv.at[g]).wait()

    def early_tile(g, t):
        total = product(g, t)
        early[t] = total if g == 0 else early[t] + total

    def early_group(g):
        y_wait(g)

        def body(t, carry):
            early_tile(g, t)
            return carry

        lax.fori_loop(0, nt, body, 0)

    order = z_order(nz, nq)
    last_of, own = {}, {}
    for n, slot in enumerate(order):
        for kind, way, d, c in slot:
            last_of[c // GROUP] = n
    lay_by = {min(last_of[g] + 8, len(order) - 1): g for g in range(groups - 1)}
    for n, slot in enumerate(order):
        for kind, way, d, c in slot:
            if d:
                z_wait(way, d, c)
            elif c not in own:
                own_rows(c)
                own[c] = n
            if kind == "send":
                z_copy(way, d, c).start()
        if n == 0:
            lax.fori_loop(0, nt, place_row, 0)
            loads[2].wait()
            lax.fori_loop(0, nt, turn, 0)
            to_scalar.wait()
        for kind, way, d, c in slot:
            if (d if way == 0 else (nz - d) % nz, c) not in done:
                pick(d if way == 0 else (nz - d) % nz, c)
        if n in lay_by:
            early_group(lay_by[n])

    def fc_copy(t):
        return pltpu.make_async_remote_copy(
            share.at[t, 1 - core], share_core.at[t], fc_send.at[t], fc_recv.at[t],
            device_id=sibling, device_id_type=MESH,
        )

    def fx_copy(t, i):
        return pltpu.make_async_remote_copy(
            share.at[t, core, lax.rem(x + i, nx)], share_x.at[t, nx - i],
            fx_send.at[t, i], fx_recv.at[t, nx - i],
            device_id=x_peer(i), device_id_type=MESH,
        )

    y_wait(groups - 1)

    def last_tile(t, carry):
        total = product(groups - 1, t)
        if groups > 1:
            total = total + early[t]
        for b in range(bands):
            share[t, b % 2, b // 2] = total[b * rows : (b + 1) * rows]
        fc_copy(t).start()
        return carry

    lax.fori_loop(0, nt, last_tile, 0)
    for t in range(nt):
        fc_copy(t).wait_recv()
        share[t, core] = share[t, core] + share_core[t]
        for i in range(1, nx):
            fx_copy(t, i).start()
    for t in range(nt):
        total = share[t, core, x]
        for i in range(1, nx):
            pltpu.make_async_copy(share_x.at[t, i], share_x.at[t, i], fx_recv.at[t, i]).wait()
            total = total + share_x[t, i]
        out[t] = total

    for u in range(units):
        core_copy(u).wait_send()
    for c in range(nq):
        for i in range(1, nx):
            x_copy(c, i).wait_send()
    for i in range(1, NY):
        want_copy(i).wait_send()
    for t in range(nt):
        fc_copy(t).wait_send()
        for i in range(1, nx):
            fx_copy(t, i).wait_send()
    for way in range(2):
        sent = sum(kind == "send" and w == way for slot in order for kind, w, _, _ in slot)
        whole = ring.at[pl.ds(0, sent // nq)]
        pltpu.make_async_copy(whole, whole, z_send.at[way]).wait()
        if sent % nq:
            some = ring.at[0, pl.ds(0, sent % nq)]
            pltpu.make_async_copy(some, some, z_send.at[way]).wait()
    whole = picked.at[:, pl.ds(1, NY - 1)]
    pltpu.make_async_copy(whole, whole, y_send).wait()


def shards(spectrum, bessel_table, interp_weights, need_owner, need_block):
    bands = lax.axis_size("band")
    nz = lax.axis_size("pair") // NY
    nx = bands // 2
    depth, radial = bessel_table.shape
    nb = spectrum.shape[1] // PB
    nt, nj, tri, local = interp_weights.shape
    nq = local // CH
    units = local // UNIT
    groups = nq // GROUP
    wide = GROUP * CH
    rows = tri // bands
    sizes = (nx, nz, nq, nb, nt, nj, tri)
    weights = jnp.swapaxes(interp_weights, 2, 3)
    dma = pltpu.SemaphoreType.DMA
    return pl.pallas_call(
        functools.partial(kernel, sizes),
        out_shape=jax.ShapeDtypeStruct((nt, rows, PB), F32),
        in_specs=[pl.BlockSpec(memory_space=pl.ANY)] * 3
        + [pl.BlockSpec(memory_space=pltpu.SMEM)] * 2,
        out_specs=pl.BlockSpec(memory_space=pltpu.VMEM),
        scratch_shapes=[
            pltpu.VMEM((depth, radial), BF16),
            pltpu.VMEM(spectrum.shape, BF16),
            pltpu.VMEM(weights.shape, BF16),
            pltpu.VMEM((units, 2, nx, UNIT, depth), BF16),
            pltpu.VMEM((groups, nt, tri, nj * wide), BF16),
            pltpu.VMEM((units, 2, nx, UNIT, nb * PB), F32),
            pltpu.VMEM((units, nx, UNIT, nb * PB), F32),
            pltpu.VMEM((nq, nx, CH, nb * PB), F32),
            pltpu.VMEM((nz, nq, nb, CH, PB), F32),
            pltpu.VMEM((2, nb, CH, PB), F32),
            pltpu.VMEM((groups, NY, nz * 2, wide, PB), F32),
            pltpu.VMEM((NY * nz * 2, wide, PB), F32),
            pltpu.VMEM((NY * nz * 2, wide, PB), F32),
            pltpu.VMEM((groups, nt, nj * wide, 2 * PB), BF16),
            pltpu.VMEM((nt, tri, PB), F32),
            pltpu.VMEM((nt, 2, nx, rows, PB), F32),
            pltpu.VMEM((nt, nx, rows, PB), F32),
            pltpu.VMEM((nt, nx, rows, PB), F32),
            pltpu.VMEM((NY, 8, PB), jnp.int32),
            pltpu.SMEM((NY, 8, PB), jnp.int32),
            pltpu.SMEM((nt * nj,), jnp.int32),
            dma((3,)),
            dma((units,)),
            dma((units,)),
            dma((nq, nx)),
            dma((nq, nx)),
            dma((2,)),
            dma((2, nz // 2 + 1, nq)),
            dma((NY,)),
            dma((NY,)),
            dma,
            dma,
            dma((groups,)),
            dma((nt,)),
            dma((nt,)),
            dma((nt, nx)),
            dma((nt, nx)),
        ],
        compiler_params=pltpu.CompilerParams(
            collective_id=0, has_side_effects=True, vmem_limit_bytes=56 * 1024 * 1024
        ),
        cost_estimate=pl.CostEstimate(flops=1 << 30, bytes_accessed=4 << 20, transcendentals=0),
    )(bessel_table, spectrum, weights, need_owner, need_block)


def solution(mesh):
    return jax.shard_map(
        shards,
        mesh=mesh,
        in_specs=(
            P("band", "pair"),
            P("band", None),
            P("pair", None, None, "band"),
            P("pair", None),
            P("pair", None),
        ),
        out_specs=P("pair", "band", None),
        check_vma=False,
    )
```

time: 355 us -> 106 us (0.30)
  waiting for transfers between devices: 268 us -> 0 us
  Pallas kernels: 0 us -> 105 us
  blocking collectives: 32.5 us -> 0 us
  starting transfers between devices: 14.4 us -> 0 us
  between operations: 14.2 us -> 0.01 us
  local copies, waits for them, and re-layouts: 13 us -> 1.47 us
  matrix products: 6.05 us -> 0 us
  other arithmetic: 5.65 us -> 0 us
    all_to_all x1 -> x0, waiting for transfers between devices: 183 us -> none  [shards(): lax.all_to_all(outgoing, 'pair', split_axis=1, concat_axis=1, tiled=True)]
    pallas_call x0 -> x1, Pallas kernels: none -> 105 us  [shards(): pl.pallas_call(functools.partial(kernel, sizes), out_shape=jax.ShapeDtype...]
    unnamed x3 -> x0, waiting for transfers between devices: 72.6 us -> none
    all_to_all x1 -> x0, blocking collectives: 32.5 us -> none  [shards(): lax.all_to_all(wanted, 'pair', split_axis=0, concat_axis=0, tiled=True)]
    all_to_all x1 -> x0, starting transfers between devices: 14.4 us -> none  [shards(): lax.all_to_all(outgoing, 'pair', split_axis=1, concat_axis=1, tiled=True)]
    reduce_scatter x1 -> x0, waiting for transfers between devices: 12.4 us -> none  [shards(): lax.psum_scatter(lax.dot_general(bessel_table, spectrum, (((0,), (0,)), (...]
    dot_general x2 -> x0, matrix products: 6.05 us -> none  [the longest x1 3.71 us: shards(): lax.dot_general(bessel_table, spectrum, (((0,), (0,)), ((), ())), preferr...]
    gather x2 -> x0, local copies, waits for them, and re-layouts: 5.59 us -> none  [the longest x1 2.8 us: shards(): picked = jnp.take(arrived, owner_flat * capacity + slot_rank, axis=1)]
  transfers between devices with their start and end apart: 3 -> 0, of which waited for: 3 -> 0; matrix products, arithmetic and copies ran while one was open for 1% -> 0% of each run, Pallas kernels for 0% -> 0%
where the time goes in v2:
time: 106 us
  Pallas kernels  105 us (99%)
  local copies, waits for them, and re-layouts  1.47 us (1%)
    pallas_call x1, Pallas kernels, shards(): pl.pallas_call(functools.partial(kernel, sizes), out_shape=jax.ShapeDtype...  105 us

profile of v2, /device:TPU:1, one launch (start us, length us, event | category | flops | bytes accessed | tf_op | source)
XLA Modules:
  0.0 106.0 jit_solution(18291428284133764337)
XLA Ops:
  0.0 104.5 %shard_map.55 = f32[4,32,128]{2,1,0:T(8,128)} custom-call(bf16[512,512]{1,0:T(8,128)(2,1)} %table_in.1, bf16[512,1536]{1,0:T(8,128)(2,1)} %spec_in.1, bf16[4,8,64,256]{3,2,1,0:T(8,128)(2,1)} %bitcast.1, s32[4,8]{1,0:T(4,128)} %owner_in.1, s32[4,8]{1,0:T(4,128)} %block_in.1), custom_call_target="tpu_custom_call" | custom-call | flops 1073741824 | bytes 4194304 | tf_op jit(solution)/shard_map/pallas_call | solution.py:361
  104.5 1.5 %copy.7 = f32[4,32,128]{2,1,0:T(8,128)} copy(f32[4,32,128]{2,1,0:T(8,128)} %shard_map.55) | data formatting | bytes 131072

commit v3 on v2

--- a/solution.py
+++ b/solution.py
@@ -12,8 +12,10 @@
 CH = 8
 UNIT = 16
 GROUP = 4
-LAG = 3
+LAG = 4
+LATE = 3
 PACE = 2
+AHEAD = 3
 MESH = pl.DeviceIdType.MESH
 F32 = jnp.float32
 BF16 = jnp.bfloat16
@@ -44,8 +46,9 @@
 
 def kernel(
     sizes,
-    table_in, spec_in, weights_in, owner_in, block_in,
+    table_in, spec_in, weights_in, owner_hbm, block_hbm,
     out,
+    owner_in, block_in,
     table, spec, weights, table_t, weights_t,
     part, core_in, band_in, ring, desk, picked, slots_0, slots_1, blocks, early,
     share, share_core, share_x,
@@ -65,6 +68,7 @@
     z, y = pair // NY, lax.rem(pair, NY)
     x, core = band // 2, lax.rem(band, 2)
     rows = tri // bands
+    x_order = sorted(range(1, nx), key=lambda i: -min(i, nx - i))
 
     def x_peer(i):
         return (pair, lax.rem(x + i, nx) * 2 + core)
@@ -75,19 +79,24 @@
     sibling = (pair, x * 2 + 1 - core)
     up = (lax.rem(z + 1, nz) * NY + y, band)
     down = (lax.rem(z + nz - 1, nz) * NY + y, band)
+
+    loads = [
+        pltpu.make_async_copy(src, dst, load_sem.at[i])
+        for i, (src, dst) in enumerate((
+            (table_in, table), (spec_in, spec), (weights_in, weights),
+            (owner_hbm, owner_in), (block_hbm, block_in),
+        ))
+    ]
+    for i in (0, 1, 3, 4, 2):
+        loads[i].start()
 
     barrier = pltpu.get_barrier_semaphore()
     partners = [x_peer(i) for i in range(1, nx)] + [y_peer(i) for i in range(1, NY)] + [up, down, sibling]
     for partner in partners:
         pl.semaphore_signal(barrier, inc=1, device_id=partner, device_id_type=MESH)
 
-    loads = [
-        pltpu.make_async_copy(src, dst, load_sem.at[i])
-        for i, (src, dst) in enumerate(((table_in, table), (spec_in, spec), (weights_in, weights)))
-    ]
-    for load in loads:
-        load.start()
-
+    loads[3].wait()
+    loads[4].wait()
     lane = lax.broadcasted_iota(jnp.int32, (8, PB), 1)
     row = lax.broadcasted_iota(jnp.int32, (8, PB), 0)
     zero = jnp.zeros((8, PB), jnp.int32)
@@ -132,12 +141,16 @@
             device_id=x_peer(i), device_id_type=MESH,
         )
 
+    def x_start(c):
+        for i in x_order:
+            x_copy(c, i).start()
+
     def across_cores(u):
         core_copy(u).wait_recv()
         part[u, core] = part[u, core] + core_in[u]
         for c in range(u * per_unit, (u + 1) * per_unit):
-            for i in range(1, nx):
-                x_copy(c, i).start()
+            if c < AHEAD:
+                x_start(c)
 
     def own_rows(c):
         for i in range(1, nx):
@@ -148,6 +161,8 @@
             total = total + band_in[c, i]
         for b in range(nb):
             ring[0, c, b] = total[:, b * PB : (b + 1) * PB]
+        if c + AHEAD < nq:
+            x_start(c + AHEAD)
 
     def want_copy(i):
         return pltpu.make_async_remote_copy(
@@ -171,25 +186,22 @@
         pltpu.make_async_copy(wants.at[i], wants.at[i], want_recv.at[i]).wait()
     to_scalar.start()
 
-    def place_row(t, carry):
+    def place_row(t):
         for j in range(nj):
             who = owner_in[t, j]
             rank = jnp.int32(0)
-            for u in range(nt - 1):
+            for u in range(t):
                 for k in range(nj):
-                    same = (owner_in[u, k] == who) & (u < t)
-                    rank = rank + same.astype(jnp.int32)
+                    rank = rank + (owner_in[u, k] == who).astype(jnp.int32)
             dz = lax.rem(z - who // NY + nz, nz)
             dy = lax.rem(lax.rem(who, NY) - y + NY, NY)
             place_s[t * nj + j] = (dy * nz + dz) * 2 + jnp.minimum(rank, 1)
-        return carry
-
-    def turn(t, carry):
+
+    def turn(t):
         for g in range(groups):
             at = g * GROUP * CH
             some = weights[t, :, at : at + GROUP * CH, :]
             weights_t[g, t] = some.reshape(nj * GROUP * CH, tri).T
-        return carry
 
     def z_copy(way, d, c):
         here = d if way == 0 else (nz - d) % nz
@@ -203,9 +215,11 @@
         here = d if way == 0 else nz - d
         pltpu.make_async_copy(ring.at[here, c], ring.at[here, c], z_recv.at[way, d, c]).wait()
 
-    def y_copy(i, g, here):
-        return pltpu.make_async_remote_copy(
-            picked.at[g, i, pl.ds(here * 2, 2)], slots[g].at[pl.ds(((NY - i) * nz + here) * 2, 2)],
+    def y_copy(i, g, here, at, count):
+        some = pl.ds(at, count)
+        return pltpu.make_async_remote_copy(
+            picked.at[g, i, pl.ds(here * 2, 2), some],
+            slots[g].at[pl.ds(((NY - i) * nz + here) * 2, 2), some],
             y_send, y_recv.at[g],
             device_id=y_peer(i), device_id_type=MESH,
         )
@@ -226,9 +240,12 @@
                     slots[g][here * 2 + s, at : at + CH] = rows_of
                 else:
                     picked[g, i, here * 2 + s, at : at + CH] = rows_of
-        if all((here, k) in done for k in range(g * GROUP, (g + 1) * GROUP)):
+        if g == groups - 1 and abs(here - nz // 2) <= LATE:
             for i in range(1, NY):
-                y_copy(i, g, here).start()
+                y_copy(i, g, here, at, CH).start()
+        elif all((here, k) in done for k in range(g * GROUP, (g + 1) * GROUP)):
+            for i in range(1, NY):
+                y_copy(i, g, here, 0, GROUP * CH).start()
 
     def product(g, t):
         for j in range(nj):
@@ -249,21 +266,13 @@
         total = product(g, t)
         early[t] = total if g == 0 else early[t] + total
 
-    def early_group(g):
-        y_wait(g)
-
-        def body(t, carry):
-            early_tile(g, t)
-            return carry
-
-        lax.fori_loop(0, nt, body, 0)
-
     order = z_order(nz, nq)
     last_of, own = {}, {}
     for n, slot in enumerate(order):
         for kind, way, d, c in slot:
             last_of[c // GROUP] = n
-    lay_by = {min(last_of[g] + 8, len(order) - 1): g for g in range(groups - 1)}
+    lay_by = {min(last_of[g] + 8 + 2 * t, len(order) - 1 - nt + t): (g, t) for g in range(groups - 1) for t in range(nt)}
+    set_up = {min(12 + 2 * t, len(order) - 1 - nt + t): t for t in range(nt)}
     for n, slot in enumerate(order):
         for kind, way, d, c in slot:
             if d:
@@ -274,15 +283,20 @@
             if kind == "send":
                 z_copy(way, d, c).start()
         if n == 0:
-            lax.fori_loop(0, nt, place_row, 0)
-            loads[2].wait()
-            lax.fori_loop(0, nt, turn, 0)
             to_scalar.wait()
         for kind, way, d, c in slot:
             if (d if way == 0 else (nz - d) % nz, c) not in done:
                 pick(d if way == 0 else (nz - d) % nz, c)
+        if n in set_up:
+            place_row(set_up[n])
+            if set_up[n] == 0:
+                loads[2].wait()
+            turn(set_up[n])
         if n in lay_by:
-            early_group(lay_by[n])
+            g, t = lay_by[n]
+            if t == 0:
+                y_wait(g)
+            early_tile(g, t)
 
     def fc_copy(t):
         return pltpu.make_async_remote_copy(
@@ -299,28 +313,18 @@
 
     y_wait(groups - 1)
 
-    def last_tile(t, carry):
+    for t in range(nt):
         total = product(groups - 1, t)
         if groups > 1:
             total = total + early[t]
         for b in range(bands):
             share[t, b % 2, b // 2] = total[b * rows : (b + 1) * rows]
         fc_copy(t).start()
-        return carry
-
-    lax.fori_loop(0, nt, last_tile, 0)
     for t in range(nt):
         fc_copy(t).wait_recv()
         share[t, core] = share[t, core] + share_core[t]
-        for i in range(1, nx):
+        for i in x_order:
             fx_copy(t, i).start()
-    for t in range(nt):
-        total = share[t, core, x]
-        for i in range(1, nx):
-            pltpu.make_async_copy(share_x.at[t, i], share_x.at[t, i], fx_recv.at[t, i]).wait()
-            total = total + share_x[t, i]
-        out[t] = total
-
     for u in range(units):
         core_copy(u).wait_send()
     for c in range(nq):
@@ -328,10 +332,6 @@
             x_copy(c, i).wait_send()
     for i in range(1, NY):
         want_copy(i).wait_send()
-    for t in range(nt):
-        fc_copy(t).wait_send()
-        for i in range(1, nx):
-            fx_copy(t, i).wait_send()
     for way in range(2):
         sent = sum(kind == "send" and w == way for slot in order for kind, w, _, _ in slot)
         whole = ring.at[pl.ds(0, sent // nq)]
@@ -341,6 +341,18 @@
             pltpu.make_async_copy(some, some, z_send.at[way]).wait()
     whole = picked.at[:, pl.ds(1, NY - 1)]
     pltpu.make_async_copy(whole, whole, y_send).wait()
+
+    for t in range(nt):
+        total = share[t, core, x]
+        for i in range(1, nx):
+            pltpu.make_async_copy(share_x.at[t, i], share_x.at[t, i], fx_recv.at[t, i]).wait()
+            total = total + share_x[t, i]
+        out[t] = total
+
+    for t in range(nt):
+        fc_copy(t).wait_send()
+        for i in range(1, nx):
+            fx_copy(t, i).wait_send()
 
 
 def shards(spectrum, bessel_table, interp_weights, need_owner, need_block):
@@ -361,10 +373,11 @@
     return pl.pallas_call(
         functools.partial(kernel, sizes),
         out_shape=jax.ShapeDtypeStruct((nt, rows, PB), F32),
-        in_specs=[pl.BlockSpec(memory_space=pl.ANY)] * 3
-        + [pl.BlockSpec(memory_space=pltpu.SMEM)] * 2,
+        in_specs=[pl.BlockSpec(memory_space=pl.ANY)] * 5,
         out_specs=pl.BlockSpec(memory_space=pltpu.VMEM),
         scratch_shapes=[
+            pltpu.SMEM(need_owner.shape, jnp.int32),
+            pltpu.SMEM(need_block.shape, jnp.int32),
             pltpu.VMEM((depth, radial), BF16),
             pltpu.VMEM(spectrum.shape, BF16),
             pltpu.VMEM(weights.shape, BF16),
@@ -386,7 +399,7 @@
             pltpu.VMEM((NY, 8, PB), jnp.int32),
             pltpu.SMEM((NY, 8, PB), jnp.int32),
             pltpu.SMEM((nt * nj,), jnp.int32),
-            dma((3,)),
+            dma((5,)),
             dma((units,)),
             dma((units,)),
             dma((nq, nx)),

time: 106 us -> 104 us (0.981)
  Pallas kernels: 105 us -> 102 us
    pallas_call x1, Pallas kernels: 105 us -> 102 us  [shards(): pl.pallas_call(functools.partial(kernel, sizes), out_shape=jax.ShapeDtype...]
where the time goes in v3:
time: 104 us; the launch traced here: 103 us
  Pallas kernels  102 us (98%)
  local copies, waits for them, and re-layouts  1.47 us (1%)
    pallas_call x1, Pallas kernels, shards(): pl.pallas_call(functools.partial(kernel, sizes), out_shape=jax.ShapeDtype...  102 us

profile of v3, /device:TPU:1, one launch (start us, length us, event | category | flops | bytes accessed | tf_op | source)
XLA Modules:
  0.0 103.4 jit_solution(14998994506679992956)
XLA Ops:
  0.0 101.9 %shard_map.55 = f32[4,32,128]{2,1,0:T(8,128)} custom-call(bf16[512,512]{1,0:T(8,128)(2,1)} %table_in.1, bf16[512,1536]{1,0:T(8,128)(2,1)} %spec_in.1, bf16[4,8,64,256]{3,2,1,0:T(8,128)(2,1)} %bitcast.1, s32[4,8]{1,0:T(4,128)} %owner_hbm.1, s32[4,8]{1,0:T(4,128)} %block_hbm.1), custom_call_target="tpu_custom_call" | custom-call | flops 1073741824 | bytes 4194304 | tf_op jit(solution)/shard_map/pallas_call | solution.py:373
  101.9 1.5 %copy.7 = f32[4,32,128]{2,1,0:T(8,128)} copy(f32[4,32,128]{2,1,0:T(8,128)} %shard_map.55) | data formatting | bytes 131072

commit v4 on v3

--- a/solution.py
+++ b/solution.py
@@ -52,13 +52,14 @@
     table, spec, weights, table_t, weights_t,
     part, core_in, band_in, ring, desk, picked, slots_0, slots_1, blocks, early,
     share, share_core, share_x,
-    wants, wants_s, place_s,
+    wants, wants_s, place_s, far_wants, far_s, far_out, far_in,
     load_sem, core_send, core_recv, x_send, x_recv, z_send, z_recv,
-    want_send, want_recv, want_local, y_send, y_recv,
+    want_send, want_recv, want_local, y_send, y_recv, fw_send, fw_recv, far_local, far_send,
     fc_send, fc_recv, fx_send, fx_recv,
 ):
     nx, nz, nq, nb, nt, nj, tri = sizes
     bands = 2 * nx
+    half = nz // 2
     units = nq * CH // UNIT
     per_unit = UNIT // CH
     groups = nq // GROUP
@@ -186,6 +187,16 @@
         pltpu.make_async_copy(wants.at[i], wants.at[i], want_recv.at[i]).wait()
     to_scalar.start()
 
+    def far_want_copy(way):
+        return pltpu.make_async_remote_copy(
+            wants, far_wants.at[1 - way], fw_send.at[way], fw_recv.at[1 - way],
+            device_id=up if way == 0 else down, device_id_type=MESH,
+        )
+
+    for way in range(2):
+        far_want_copy(way).start()
+    to_far = pltpu.make_async_copy(far_wants, far_s, far_local)
+
     def place_row(t):
         for j in range(nj):
             who = owner_in[t, j]
@@ -213,7 +224,36 @@
 
     def z_wait(way, d, c):
         here = d if way == 0 else nz - d
-        pltpu.make_async_copy(ring.at[here, c], ring.at[here, c], z_recv.at[way, d, c]).wait()
+        what = far_in.at[c] if d == half else ring.at[here, c]
+        pltpu.make_async_copy(what, what, z_recv.at[way, d, c]).wait()
+
+    def far_copy(way, c):
+        return pltpu.make_async_remote_copy(
+            far_out.at[c], far_in.at[c], far_send, z_recv.at[way, half, c],
+            device_id=up if way == 0 else down, device_id_type=MESH,
+        )
+
+    def far_go(way, c):
+        here = half - 1 if way == 0 else nz - half + 1
+        desk[2] = ring[here, c]
+        who = lax.rem(z + nz - here, nz) * NY + y
+        for i in range(NY):
+            for s in range(2):
+                far_out[c, i * 2 + s] = desk[2, far_s[way, i, s, who]]
+        far_copy(way, c).start()
+
+    def far_come(c):
+        g = c // GROUP
+        at = c % GROUP * CH
+        done[half, c] = True
+        slots[g][half * 2 : half * 2 + 2, at : at + CH] = far_in[c, 0:2]
+        for i in range(1, NY):
+            pltpu.make_async_remote_copy(
+                far_in.at[c, pl.ds(i * 2, 2)],
+                slots[g].at[pl.ds(((NY - i) * nz + half) * 2, 2), pl.ds(at, CH)],
+                y_send, y_recv.at[g],
+                device_id=y_peer(i), device_id_type=MESH,
+            ).start()
 
     def y_copy(i, g, here, at, count):
         some = pl.ds(at, count)
@@ -267,7 +307,7 @@
         early[t] = total if g == 0 else early[t] + total
 
     order = z_order(nz, nq)
-    last_of, own = {}, {}
+    last_of, own, far_ready = {}, {}, []
     for n, slot in enumerate(order):
         for kind, way, d, c in slot:
             last_of[c // GROUP] = n
@@ -280,12 +320,22 @@
             elif c not in own:
                 own_rows(c)
                 own[c] = n
-            if kind == "send":
+            if kind == "send" and d == half - 1:
+                if not far_ready:
+                    for w in range(2):
+                        pltpu.make_async_copy(far_wants.at[w], far_wants.at[w], fw_recv.at[w]).wait()
+                    to_far.start()
+                    to_far.wait()
+                    far_ready.append(n)
+                far_go(way, c)
+            elif kind == "send":
                 z_copy(way, d, c).start()
         if n == 0:
             to_scalar.wait()
         for kind, way, d, c in slot:
-            if (d if way == 0 else (nz - d) % nz, c) not in done:
+            if d == half:
+                far_come(c)
+            elif (d if way == 0 else (nz - d) % nz, c) not in done:
                 pick(d if way == 0 else (nz - d) % nz, c)
         if n in set_up:
             place_row(set_up[n])
@@ -333,12 +383,14 @@
     for i in range(1, NY):
         want_copy(i).wait_send()
     for way in range(2):
-        sent = sum(kind == "send" and w == way for slot in order for kind, w, _, _ in slot)
+        far_want_copy(way).wait_send()
+        sent = sum(kind == "send" and w == way and d < half - 1 for slot in order for kind, w, d, _ in slot)
         whole = ring.at[pl.ds(0, sent // nq)]
         pltpu.make_async_copy(whole, whole, z_send.at[way]).wait()
         if sent % nq:
             some = ring.at[0, pl.ds(0, sent % nq)]
             pltpu.make_async_copy(some, some, z_send.at[way]).wait()
+    pltpu.make_async_copy(far_out, far_out, far_send).wait()
     whole = picked.at[:, pl.ds(1, NY - 1)]
     pltpu.make_async_copy(whole, whole, y_send).wait()
 
@@ -387,7 +439,7 @@
             pltpu.VMEM((units, nx, UNIT, nb * PB), F32),
             pltpu.VMEM((nq, nx, CH, nb * PB), F32),
             pltpu.VMEM((nz, nq, nb, CH, PB), F32),
-            pltpu.VMEM((2, nb, CH, PB), F32),
+            pltpu.VMEM((3, nb, CH, PB), F32),
             pltpu.VMEM((groups, NY, nz * 2, wide, PB), F32),
             pltpu.VMEM((NY * nz * 2, wide, PB), F32),
             pltpu.VMEM((NY * nz * 2, wide, PB), F32),
@@ -399,6 +451,10 @@
             pltpu.VMEM((NY, 8, PB), jnp.int32),
             pltpu.SMEM((NY, 8, PB), jnp.int32),
             pltpu.SMEM((nt * nj,), jnp.int32),
+            pltpu.VMEM((2, NY, 8, PB), jnp.int32),
+            pltpu.SMEM((2, NY, 8, PB), jnp.int32),
+            pltpu.VMEM((nq, NY * 2, CH, PB), F32),
+            pltpu.VMEM((nq, NY * 2, CH, PB), F32),
             dma((5,)),
             dma((units,)),
             dma((units,)),
@@ -411,6 +467,10 @@
             dma,
             dma,
             dma((groups,)),
+            dma((2,)),
+            dma((2,)),
+            dma,
+            dma,
             dma((nt,)),
             dma((nt,)),
             dma((nt, nx)),

time: 104 us -> 103 us (level)
  no operation moved by 1% of the time
where the time goes in v4:
time: 103 us
  Pallas kernels  102 us (99%)
  local copies, waits for them, and re-layouts  1.47 us (1%)
    pallas_call x1, Pallas kernels, shards(): pl.pallas_call(functools.partial(kernel, sizes), out_shape=jax.ShapeDtype...  102 us

profile of v4, /device:TPU:1, one launch (start us, length us, event | category | flops | bytes accessed | tf_op | source)
XLA Modules:
  0.0 103.0 jit_solution(12107790517024446832)
XLA Ops:
  0.0 101.5 %shard_map.55 = f32[4,32,128]{2,1,0:T(8,128)} custom-call(bf16[512,512]{1,0:T(8,128)(2,1)} %table_in.1, bf16[512,1536]{1,0:T(8,128)(2,1)} %spec_in.1, bf16[4,8,64,256]{3,2,1,0:T(8,128)(2,1)} %bitcast.1, s32[4,8]{1,0:T(4,128)} %owner_hbm.1, s32[4,8]{1,0:T(4,128)} %block_hbm.1), custom_call_target="tpu_custom_call" | custom-call | flops 1073741824 | bytes 4194304 | tf_op jit(solution)/shard_map/pallas_call | solution.py:425
  101.5 1.5 %copy.7 = f32[4,32,128]{2,1,0:T(8,128)} copy(f32[4,32,128]{2,1,0:T(8,128)} %shard_map.55) | data formatting | bytes 131072

commit v5 on v4

--- a/solution.py
+++ b/solution.py
@@ -12,7 +12,7 @@
 CH = 8
 UNIT = 16
 GROUP = 4
-LAG = 4
+LAG = 5
 LATE = 3
 PACE = 2
 AHEAD = 3
@@ -69,6 +69,7 @@
     z, y = pair // NY, lax.rem(pair, NY)
     x, core = band // 2, lax.rem(band, 2)
     rows = tri // bands
+    y_order = sorted(range(1, NY), key=lambda i: -min(i, NY - i))
     x_order = sorted(range(1, nx), key=lambda i: -min(i, nx - i))
 
     def x_peer(i):
@@ -247,7 +248,7 @@
         at = c % GROUP * CH
         done[half, c] = True
         slots[g][half * 2 : half * 2 + 2, at : at + CH] = far_in[c, 0:2]
-        for i in range(1, NY):
+        for i in y_order:
             pltpu.make_async_remote_copy(
                 far_in.at[c, pl.ds(i * 2, 2)],
                 slots[g].at[pl.ds(((NY - i) * nz + half) * 2, 2), pl.ds(at, CH)],
@@ -281,10 +282,10 @@
                 else:
                     picked[g, i, here * 2 + s, at : at + CH] = rows_of
         if g == groups - 1 and abs(here - nz // 2) <= LATE:
-            for i in range(1, NY):
+            for i in y_order:
                 y_copy(i, g, here, at, CH).start()
         elif all((here, k) in done for k in range(g * GROUP, (g + 1) * GROUP)):
-            for i in range(1, NY):
+            for i in y_order:
                 y_copy(i, g, here, 0, GROUP * CH).start()
 
     def product(g, t):

time: 103 us -> 103 us (level)
  no operation moved by 1% of the time
where the time goes in v5:
time: 103 us
  Pallas kernels  101 us (98%)
  local copies, waits for them, and re-layouts  1.47 us (1%)
    pallas_call x1, Pallas kernels, shards(): pl.pallas_call(functools.partial(kernel, sizes), out_shape=jax.ShapeDtype...  101 us

profile of v5, /device:TPU:1, one launch (start us, length us, event | category | flops | bytes accessed | tf_op | source)
XLA Modules:
  0.0 102.5 jit_solution(14126005605318561953)
XLA Ops:
  0.0 101.1 %shard_map.55 = f32[4,32,128]{2,1,0:T(8,128)} custom-call(bf16[512,512]{1,0:T(8,128)(2,1)} %table_in.1, bf16[512,1536]{1,0:T(8,128)(2,1)} %spec_in.1, bf16[4,8,64,256]{3,2,1,0:T(8,128)(2,1)} %bitcast.1, s32[4,8]{1,0:T(4,128)} %owner_hbm.1, s32[4,8]{1,0:T(4,128)} %block_hbm.1), custom_call_target="tpu_custom_call" | custom-call | flops 1073741824 | bytes 4194304 | tf_op jit(solution)/shard_map/pallas_call | solution.py:426
  101.1 1.5 %copy.7 = f32[4,32,128]{2,1,0:T(8,128)} copy(f32[4,32,128]{2,1,0:T(8,128)} %shard_map.55) | data formatting | bytes 131072

commit v6 on v5

--- a/solution.py
+++ b/solution.py
@@ -12,7 +12,7 @@
 CH = 8
 UNIT = 16
 GROUP = 4
-LAG = 5
+LAG = 6
 LATE = 3
 PACE = 2
 AHEAD = 3

time: 103 us -> 104 us (level)
    pallas_call x1, Pallas kernels: 101 us -> 102 us  [shards(): pl.pallas_call(functools.partial(kernel, sizes), out_shape=jax.ShapeDtype...]
where the time goes in v6:
time: 104 us
  Pallas kernels  102 us (98%)
  local copies, waits for them, and re-layouts  1.47 us (1%)
    pallas_call x1, Pallas kernels, shards(): pl.pallas_call(functools.partial(kernel, sizes), out_shape=jax.ShapeDtype...  102 us

profile of v6, /device:TPU:1, one launch (start us, length us, event | category | flops | bytes accessed | tf_op | source)
XLA Modules:
  0.0 103.7 jit_solution(4879546006715030748)
XLA Ops:
  0.0 102.3 %shard_map.55 = f32[4,32,128]{2,1,0:T(8,128)} custom-call(bf16[512,512]{1,0:T(8,128)(2,1)} %table_in.1, bf16[512,1536]{1,0:T(8,128)(2,1)} %spec_in.1, bf16[4,8,64,256]{3,2,1,0:T(8,128)(2,1)} %bitcast.1, s32[4,8]{1,0:T(4,128)} %owner_hbm.1, s32[4,8]{1,0:T(4,128)} %block_hbm.1), custom_call_target="tpu_custom_call" | custom-call | flops 1073741824 | bytes 4194304 | tf_op jit(solution)/shard_map/pallas_call | solution.py:426
  102.3 1.5 %copy.7 = f32[4,32,128]{2,1,0:T(8,128)} copy(f32[4,32,128]{2,1,0:T(8,128)} %shard_map.55) | data formatting | bytes 131072
